TPU v7x, 128 devices: a whole 4x4x4 slice. The times are simulated.
128 devices in a mesh: grid: 64 (over x, y, z_lo, core), col: 2 (over z_hi).
Axes of the slice: x: 4, y: 4, z: 4 (z_hi: 2, z_lo: 2; z = z_hi * 2 + z_lo), core: 2. Of those that a mesh axis runs over, the one named last changes fastest.
Arguments:
- orbitals: bfloat16 [884736, 256], P(('grid', 'col')), may hold values from -6 to 6
- points: int32 [1024], replicated, may hold values from 0 to 884735, as said below
- cinv: bfloat16 [1024, 256], replicated, may hold values from -0.1875 to 0.1875
Outputs:
- potential: bfloat16 [256, 884736], P(None, ('grid', 'col'))
- coupling: float32 [1024, 256], P(('grid', 'col'))
Inputs may be any that keep to these rules, and one draw needn't show every extreme that they name: `points`: 1024 distinct grid rows.
All inputs are finite; a program needn't handle non-finite values.
Results may differ from a plain program's by a relative error of at most 0.0046.
Values may be sent and summed in bfloat16 or wider, within the bound.
A program may use at most 192 MiB of HBM per device.

v0:
```python
import math
import jax
import jax.numpy as jnp
from jax import lax
from jax.sharding import PartitionSpec as P

NX = 96
screening = 0.25


def kernel_table(size):
    index = jnp.arange(size)
    wave = jnp.where(index < (size + 1) // 2, index, index - size).astype(jnp.float32) * (
        2.0 * math.pi / size
    )
    squared = wave[:, None, None] ** 2 + wave[None, :, None] ** 2 + wave[None, None, :] ** 2
    return jnp.where(squared > 0, 1.0 / (squared + screening), 0.0)


def along(table, values, axis):
    forms = {1: "kn,cnyz->ckyz", 2: "kn,cxnz->cxkz", 3: "kn,cxyn->cxyk"}
    return jnp.einsum(forms[axis], table, values, precision=lax.Precision.HIGHEST)


def screened_solve(field):
    size = field.shape[1]
    index = jnp.arange(size, dtype=jnp.int32)
    phase = index[:, None] * index[None, :] % size
    angle = phase.astype(jnp.float32) * (2.0 * math.pi / size)
    cos_table = jnp.cos(angle)
    sin_table = jnp.sin(angle)
    real_part = along(cos_table, field, 3)
    imag_part = -along(sin_table, field, 3)
    for axis in (2, 1):
        real_part, imag_part = (
            along(cos_table, real_part, axis) + along(sin_table, imag_part, axis),
            along(cos_table, imag_part, axis) - along(sin_table, real_part, axis),
        )
    weights = kernel_table(size)
    real_part = real_part * weights
    imag_part = imag_part * weights
    for axis in (1, 2):
        real_part, imag_part = (
            along(cos_table, real_part, axis) - along(sin_table, imag_part, axis),
            along(cos_table, imag_part, axis) + along(sin_table, real_part, axis),
        )
    result = along(cos_table, real_part, 3) - along(sin_table, imag_part, 3)
    return result / float(size**3)


def local(orbitals, points, cinv):
    ranks = lax.axis_size(("grid", "col"))
    local_rows = orbitals.shape[0]
    orbital_count = orbitals.shape[1]
    npoints = cinv.shape[0]
    columns = cinv.shape[1]
    per_rank = columns // ranks
    first_row = lax.axis_index(("grid", "col")) * local_rows
    offset = points - first_row
    inside = (offset >= 0) & (offset < local_rows)
    picked = jnp.take(orbitals, jnp.clip(offset, 0, local_rows - 1), axis=0)
    picked = jnp.where(inside[:, None], picked.astype(jnp.float32), 0.0)
    point_rows = lax.psum(picked, ("grid", "col")).astype(jnp.bfloat16)
    scale = 1.0 / math.sqrt(orbital_count)
    block_rows = math.gcd(local_rows, 1152)

    def pair_block(block):
        product = (
            lax.dot_general(
                block, point_rows, (((1,), (1,)), ((), ())), preferred_element_type=jnp.float32
            )
            * scale
        )
        return (product * product).astype(jnp.bfloat16)

    pairs = lax.map(
        pair_block, orbitals.reshape(local_rows // block_rows, block_rows, orbital_count)
    )
    pairs = pairs.reshape(local_rows, npoints)
    theta_cols = lax.dot_general(
        cinv, pairs, (((0,), (1,)), ((), ())), preferred_element_type=jnp.float32
    )
    fields = lax.all_to_all(theta_cols, ("grid", "col"), split_axis=0, concat_axis=1, tiled=True)
    fields = fields.reshape(per_rank, NX, NX, NX)
    potentials = screened_solve(fields).astype(jnp.bfloat16).reshape(per_rank, NX * NX * NX)
    rows_back = lax.all_to_all(potentials, ("grid", "col"), split_axis=1, concat_axis=0, tiled=True)
    factor = math.sqrt(npoints) / float(NX**3)
    coupling = lax.psum_scatter(
        lax.dot_general(
            pairs, rows_back, (((0,), (1,)), ((), ())), preferred_element_type=jnp.float32
        )
        * factor,
        ("grid", "col"),
        scatter_dimension=0,
        tiled=True,
    )
    return (rows_back, coupling)


def solution(mesh):
    in_specs = (P(("grid", "col"), None), P(), P())
    out_specs = (P(None, ("grid", "col")), P(("grid", "col"), None))
    return jax.shard_map(local, mesh=mesh, in_specs=in_specs, out_specs=out_specs, check_vma=False)
```

profile of v0, /device:TPU:0, one launch (start us, length us, event | category | flops | bytes accessed | tf_op | source)
XLA Modules:
  0.0 1324.5 jit_solution(9655108853187020111)
XLA Ops:
  7.2 0.8 compare_and_fusion.1
  7.9 0.7 fusion.144
  8.6 5.9 gather_fusion
  14.9 74.1 %all-reduce.1 = bf16[1024,256]{1,0:T(8,128)(2,1)S(1)} all-reduce(f32[1024,256]{1,0:T(8,128)S(1)} %convert_select_fusion), channel_id=1, replica_groups=mesh['grid'=64,'col'=2] {'grid','col'}, use_global_device_ids=true, to_apply=%region_0.1 | all-reduce | flops 262144 | bytes 1572864 | tf_op jit(solution)/shard_map/psum | solution.py:63
  89.0 19.9 %while.10 = (s32[]{:T(128)}, bf16[6,1152,1024]{2,1,0:T(8,128)(2,1)}, bf16[6,1152,256]{2,1,0:T(8,128)(2,1)}, bf16[1024,256]{1,0:T(8,128)(2,1)S(1)}, s32[]{:T(128)}) while((s32[]{:T(128)}, bf16[6,1152,1024]{2,1,0:T(8,128)(2,1)}, bf16[6,1152,256]{2,1,0:T(8,128)(2,1)}, bf16[1024,256]{1,0:T(8,128)(2,1)S(1)}, s32[]{:T(128)}) %tuple.28), condition=%wide.region_2.3_spmd, body=%wide.region_1.2_spmd.sunk | while | flops 607518720 | bytes 3474501 | solution.py:76
  89.0 3.3 fusion.234
  92.3 3.3 fusion.234
  95.7 3.3 fusion.234
  99.0 3.4 fusion.234
  102.3 3.3 fusion.234
  105.6 3.3 fusion.234
  109.0 11.7 convolution_bitcast_fusion
  120.7 9.1 all_to_all.26
  129.8 6.9 all-to-all-start
  137.1 3.1 fusion.18
  140.1 81.1 %all-to-all-done = f32[128,2,6912]{2,1,0:T(2,128)} async-done(((f32[128,2,6912]{2,1,0:T(2,128)}), f32[128,2,6912]{2,1,0:T(2,128)}, u32[]{:S(2)}, u32[]{:S(2)}) %all-to-all-start) | async-done | bytes 7077920 | tf_op jit(solution)/shard_map/all_to_all | solution.py:83
  221.2 6.4 copy.15
  227.6 10.6 reshape.103
  238.2 11.3 fusion.39
  249.5 21.2 %fusion.57 = f32[2,96,96,96]{2,3,1,0:T(8,128)S(1)} fusion(f32[2,96,96,96]{3,2,1,0:T(8,128)S(1)} %copy-done.6), kind=kOutput, calls=%fused_computation.66 | convolution fusion | flops 2038514688 | bytes 14155776 | tf_op jit(solution)/shard_map/kn,cxyn->cxyk/dot_general | solution.py:22
  270.7 8.8 fusion.55
  279.5 10.5 fusion.36
  290.0 19.2 %subtract_bitcast_fusion.1 = f32[2,96,96,96]{2,3,1,0:T(8,128)} fusion(f32[2,96,96,96]{3,2,1,0:T(8,128)} %fusion.36, f32[2,96,96,96]{3,2,1,0:T(8,128)S(1)} %fusion.39), kind=kOutput, calls=%fused_computation.21 | convolution fusion | flops 2042053632 | bytes 21233664 | tf_op jit(solution)/shard_map/kn,cxnz->cxkz/dot_general | solution.py:22
  309.2 17.8 %add_bitcast_fusion.1 = f32[2,96,96,96]{2,3,1,0:T(8,128)} fusion(f32[2,96,96,96]{3,2,1,0:T(8,128)S(1)} %fusion.55, f32[2,96,96,96]{3,2,1,0:T(8,128)S(1)} %fusion.39), kind=kOutput, calls=%fused_computation.22 | convolution fusion | flops 2042053632 | bytes 21233664 | tf_op jit(solution)/shard_map/kn,cxnz->cxkz/dot_general | solution.py:22
  326.9 12.4 copy.18
  339.3 12.4 copy.21
  351.7 13.4 %fusion.48 = f32[2,96,96,96]{3,2,1,0:T(8,128)} fusion(f32[2,96,96,96]{1,3,2,0:T(8,128)} %copy.21), kind=kOutput, calls=%fused_computation.57 | convolution fusion | flops 2038514688 | bytes 14155776 | tf_op jit(solution)/shard_map/kn,cnyz->ckyz/dot_general | solution.py:22
  365.1 10.2 fusion.53
  375.3 11.3 bitcast_multiply_fusion
  386.6 15.4 %bitcast_multiply_fusion.1 = f32[2,96,96,96]{1,3,2,0:T(8,128)S(1)} fusion(f32[2,96,96,96]{3,2,1,0:T(8,128)} %fusion.53, f32[96,96,96]{0,2,1:T(8,128)S(1)} %bitcast.109, f32[2,96,96,96]{1,3,2,0:T(8,128)} %copy.21), kind=kOutput, calls=%fused_computation.15 | convolution fusion | flops 2042053632 | bytes 24772608 | tf_op jit(solution)/shard_map/kn,cnyz->ckyz/dot_general | solution.py:22
  402.0 10.3 fusion.50
  412.3 8.8 fusion.44
  421.1 10.6 add_bitcast_fusion
  431.7 12.4 copy.31
  444.1 26.4 %fusion.41 = f32[2,96,96,96]{2,3,1,0:T(8,128)} fusion(f32[2,96,96,96]{2,3,1,0:T(8,128)} %copy.31), kind=kOutput, calls=%fused_computation.50 | convolution fusion | flops 2038514688 | bytes 14155776 | tf_op jit(solution)/shard_map/kn,cxnz->cxkz/dot_general | solution.py:22
  470.6 23.6 %fusion.30 = f32[2,96,96,96]{2,3,1,0:T(8,128)} fusion(f32[2,96,96,96]{2,3,1,0:T(8,128)S(1)} %copy-done.3), kind=kOutput, calls=%fused_computation.39 | convolution fusion | flops 2038514688 | bytes 14155776 | tf_op jit(solution)/shard_map/kn,cxnz->cxkz/dot_general | solution.py:22
  494.3 10.6 subtract_bitcast_fusion
  504.8 12.5 copy.30
  517.4 24.6 %fusion.28 = f32[2,96,96,96]{2,3,1,0:T(8,128)S(1)} fusion(f32[2,96,96,96]{2,3,1,0:T(8,128)} %copy.30), kind=kOutput, calls=%fused_computation.37 | convolution fusion | flops 2038514688 | bytes 14155776 | tf_op jit(solution)/shard_map/kn,cxnz->cxkz/dot_general | solution.py:22
  542.0 23.4 %fusion.46 = f32[2,96,96,96]{2,3,1,0:T(8,128)} fusion(f32[2,96,96,96]{2,3,1,0:T(8,128)S(1)} %copy-done.4), kind=kOutput, calls=%fused_computation.55 | convolution fusion | flops 2038514688 | bytes 14155776 | tf_op jit(solution)/shard_map/kn,cxnz->cxkz/dot_general | solution.py:22
  565.4 10.2 fusion.7
  575.6 15.9 %multiply_convert_fusion = bf16[2,96,96,96]{3,2,1,0:T(8,128)(2,1)} fusion(f32[2,96,96,96]{3,2,1,0:T(8,128)} %fusion.7, f32[2,96,96,96]{2,3,1,0:T(8,128)} %fusion.46, f32[2,96,96,96]{2,3,1,0:T(8,128)} %fusion.30), kind=kOutput, calls=%fused_computation.16 | convolution fusion | flops 2045592576 | bytes 24772608 | tf_op jit(solution)/shard_map/kn,cxyn->cxyk/dot_general | solution.py:22
  591.5 7.8 all_to_all.29
  599.3 5.6 copy.24
  604.9 55.8 %all_to_all.35 = bf16[2,128,6912]{2,0,1:T(2,128)(2,1)} all-to-all(bf16[2,128,6912]{2,0,1:T(2,128)(2,1)S(1)} %copy.24), channel_id=1, replica_groups=mesh['grid'=64,'col'=2] {'grid','col'}, dimensions={1} | all-to-all | bytes 7077888 | tf_op jit(solution)/shard_map/all_to_all | solution.py:86
  660.7 8.3 all_to_all.32
  669.0 10.9 convolution_multiply_fusion.1
  679.9 637.2 %reduce-scatter.2.cloned.1.call-done = f32[8,256]{1,0:T(8,128)} async-done(((f32[1024,256]{1,0:T(8,128)}), f32[8,256]{1,0:T(8,128)}) %reduce-scatter.2.cloned.1.call-update) | async-done | bytes 8208 | tf_op jit(solution)/shard_map/reduce_scatter | solution.py:88
  (46 shorter events, 0.8 us)
Async XLA Ops:
  7.2 101.8 %copy-start = (bf16[1024,256]{1,0:T(8,128)(2,1)S(1)}, bf16[1024,256]{1,0:T(8,128)(2,1)}, u32[]{:S(2)}) copy-start(bf16[1024,256]{1,0:T(8,128)(2,1)} %param.7) | copy-start | bytes 1572868
  129.8 91.4 %all-to-all-start = ((f32[128,2,6912]{2,1,0:T(2,128)}), f32[128,2,6912]{2,1,0:T(2,128)}, u32[]{:S(2)}, u32[]{:S(2)}) async-start(f32[128,2,6912]{2,1,0:T(2,128)} %all_to_all.26), calls=%async_computation | async-start | bytes 14155776 | tf_op jit(solution)/shard_map/all_to_all | solution.py:83
  136.7 1180.5 %reduce-scatter.2.cloned.1.call-start = ((), (), s32[]{:S(2)}) async-start(), calls=%async_computation.3 | async-start | bytes 1056768 | tf_op jit(solution)/shard_map/reduce_scatter | solution.py:88
  238.2 11.3 copy-start.6
  351.7 13.4 %copy-start.5 = (f32[2,96,96,96]{1,3,2,0:T(8,128)S(1)}, f32[2,96,96,96]{1,3,2,0:T(8,128)}, u32[]{:S(2)}) copy-start(f32[2,96,96,96]{1,3,2,0:T(8,128)} %copy.18) | copy-start | bytes 21233668
  351.7 23.6 %slice-start = ((s8[4718592]{0:T(1024)(128)(4,1)}), s8[4194304]{0:T(1024)(128)(4,1)S(1)}, s32[]{:S(2)}) async-start(s8[4718592]{0:T(1024)(128)(4,1)} %bitcast.108), calls=%async_computation.4 | async-start | bytes 8388608
  365.1 10.2 slice-start.1
  386.6 25.7 %copy-start.2 = (f32[2,96,96,96]{1,3,2,0:T(8,128)}, f32[2,96,96,96]{1,3,2,0:T(8,128)S(1)}, u32[]{:S(2)}) copy-start(f32[2,96,96,96]{1,3,2,0:T(8,128)S(1)} %bitcast_multiply_fusion) | copy-start | bytes 21233668
  444.1 26.4 %copy-start.3 = (f32[2,96,96,96]{2,3,1,0:T(8,128)S(1)}, f32[2,96,96,96]{2,3,1,0:T(8,128)}, u32[]{:S(2)}) copy-start(f32[2,96,96,96]{2,3,1,0:T(8,128)} %copy.31) | copy-start | bytes 21233668
  444.1 50.1 %slice-start.2 = ((s8[9437184]{0:T(1024)(128)(4,1)}), s8[4194304]{0:T(1024)(128)(4,1)S(1)}, s32[]{:S(2)}) async-start(s8[9437184]{0:T(1024)(128)(4,1)} %bitcast.110), calls=%async_computation.6 | async-start | bytes 8388608
  444.1 50.1 %slice-start.3 = ((s8[9437184]{0:T(1024)(128)(4,1)}), s8[4194304]{0:T(1024)(128)(4,1)S(1)}, s32[]{:S(2)}) async-start(s8[9437184]{0:T(1024)(128)(4,1)} %bitcast.110), calls=%async_computation.7 | async-start | bytes 8388608
  444.1 50.1 %slice-start.5 = ((s8[9437184]{0:T(1024)(128)(4,1)}), s8[4194304]{0:T(1024)(128)(4,1)S(1)}, s32[]{:S(2)}) async-start(s8[9437184]{0:T(1024)(128)(4,1)} %bitcast.112), calls=%async_computation.9 | async-start | bytes 8388608
  444.1 50.1 %slice-start.6 = ((s8[9437184]{0:T(1024)(128)(4,1)}), s8[4194304]{0:T(1024)(128)(4,1)S(1)}, s32[]{:S(2)}) async-start(s8[9437184]{0:T(1024)(128)(4,1)} %bitcast.112), calls=%async_computation.10 | async-start | bytes 8388608
  470.6 23.7 %slice-start.4 = ((s8[9437184]{0:T(1024)(128)(4,1)}), s8[1048576]{0:T(1024)(128)(4,1)S(1)}, s32[]{:S(2)}) async-start(s8[9437184]{0:T(1024)(128)(4,1)} %bitcast.110), calls=%async_computation.8 | async-start | bytes 2097152
  470.6 23.7 %slice-start.7 = ((s8[9437184]{0:T(1024)(128)(4,1)}), s8[1048576]{0:T(1024)(128)(4,1)S(1)}, s32[]{:S(2)}) async-start(s8[9437184]{0:T(1024)(128)(4,1)} %bitcast.112), calls=%async_computation.11 | async-start | bytes 2097152
  517.4 24.6 %copy-start.4 = (f32[2,96,96,96]{2,3,1,0:T(8,128)S(1)}, f32[2,96,96,96]{2,3,1,0:T(8,128)}, u32[]{:S(2)}) copy-start(f32[2,96,96,96]{2,3,1,0:T(8,128)} %copy.30) | copy-start | bytes 21233668
  517.4 48.0 %slice-start.8 = ((s8[9437184]{0:T(1024)(128)(4,1)}), s8[4194304]{0:T(1024)(128)(4,1)S(1)}, s32[]{:S(2)}) async-start(s8[9437184]{0:T(1024)(128)(4,1)} %bitcast.114), calls=%async_computation.12 | async-start | bytes 8388608
  517.4 48.0 %slice-start.9 = ((s8[9437184]{0:T(1024)(128)(4,1)}), s8[4194304]{0:T(1024)(128)(4,1)S(1)}, s32[]{:S(2)}) async-start(s8[9437184]{0:T(1024)(128)(4,1)} %bitcast.114), calls=%async_computation.13 | async-start | bytes 8388608
  542.0 23.4 %slice-start.10 = ((s8[9437184]{0:T(1024)(128)(4,1)}), s8[1048576]{0:T(1024)(128)(4,1)S(1)}, s32[]{:S(2)}) async-start(s8[9437184]{0:T(1024)(128)(4,1)} %bitcast.114), calls=%async_computation.14 | async-start | bytes 2097152
  660.7 656.4 %copy-start.1 = (bf16[1024,256]{1,0:T(8,128)(2,1)S(1)}, bf16[1024,256]{1,0:T(8,128)(2,1)}, u32[]{:S(2)}) copy-start(bf16[1024,256]{1,0:T(8,128)(2,1)} %param.7) | copy-start | bytes 1572868
Sparse Core Ops, SparseCore 0:
  680.1 637.0 reduce-scatter.1
where the time goes:
time: 1330 us; the launch traced here: 1320 us
  waiting for transfers between devices  718 us (54%)
  matrix products  346 us (26%)
  blocking collectives  130 us (10%)
  local copies, waits for them, and re-layouts  103 us (8%)
  between operations  14.8 us (1%)
    reduce_scatter x1, waiting for transfers between devices, local(): lax.psum_scatter(lax.dot_general(pairs, rows_back, (((0,), (1,)), ((), ()...  637 us
    dot_general x20, matrix products, along(): jnp.einsum(forms[axis], table, values, precision=lax.Precision.HIGHEST)  303 us
    all_to_all x1, waiting for transfers between devices, local(): lax.all_to_all(theta_cols, ('grid', 'col'), split_axis=0, concat_axis=1,...  81.1 us
    psum x1, blocking collectives, local(): point_rows = lax.psum(picked, ('grid', 'col')).astype(jnp.bfloat16)  74.1 us
    all_to_all x1, blocking collectives, local(): lax.all_to_all(potentials, ('grid', 'col'), split_axis=1, concat_axis=0,...  55.8 us
  transfers between devices with their start and end apart: 2, of which 2 were waited for; matrix products, arithmetic and copies ran while one was open for 0% of the time, Pallas kernels for 0%

commit v1 on v0

--- a/solution.py
+++ b/solution.py
@@ -6,6 +6,12 @@
 
 NX = 96
 screening = 0.25
+
+
+def _launch_series(message):
+    mat_out = lax.psum(message, axis_name="grid")
+    moved = lax.psum(mat_out, axis_name="col")
+    return moved
 
 
 def kernel_table(size):
@@ -60,7 +66,7 @@
     inside = (offset >= 0) & (offset < local_rows)
     picked = jnp.take(orbitals, jnp.clip(offset, 0, local_rows - 1), axis=0)
     picked = jnp.where(inside[:, None], picked.astype(jnp.float32), 0.0)
-    point_rows = lax.psum(picked, ("grid", "col")).astype(jnp.bfloat16)
+    point_rows = _launch_series(picked).astype(jnp.bfloat16)
     scale = 1.0 / math.sqrt(orbital_count)
     block_rows = math.gcd(local_rows, 1152)
 

time: 1330 us -> 1840 us (1.38)
  waiting for transfers between devices: 718 us -> 1270 us
  blocking collectives: 130 us -> 87.8 us
    psum x0 -> x1, waiting for transfers between devices: none -> 549 us  [_launch_series(): mat_out = lax.psum(message, axis_name='grid')]
    psum x1, blocking collectives: 74.1 us -> 32 us  [_launch_series(): moved = lax.psum(mat_out, axis_name='col')]
  transfers between devices with their start and end apart: 2 -> 3, of which waited for: 2 -> 3; matrix products, arithmetic and copies ran while one was open for 0% -> 0% of each run, Pallas kernels for 0% -> 0%
where the time goes in v1:
time: 1840 us
  waiting for transfers between devices  1270 us (69%)
  matrix products  346 us (19%)
  local copies, waits for them, and re-layouts  103 us (6%)
  blocking collectives  87.8 us (5%)
    reduce_scatter x1, waiting for transfers between devices, local(): lax.psum_scatter(lax.dot_general(pairs, rows_back, (((0,), (1,)), ((), ()...  637 us
    psum x1, waiting for transfers between devices, _launch_series(): mat_out = lax.psum(message, axis_name='grid')  549 us
    dot_general x20, matrix products, along(): jnp.einsum(forms[axis], table, values, precision=lax.Precision.HIGHEST)  303 us
    all_to_all x1, waiting for transfers between devices, local(): lax.all_to_all(theta_cols, ('grid', 'col'), split_axis=0, concat_axis=1,...  81.1 us
    all_to_all x1, blocking collectives, local(): lax.all_to_all(potentials, ('grid', 'col'), split_axis=1, concat_axis=0,...  55.8 us
  transfers between devices with their start and end apart: 3, of which 3 were waited for; matrix products, arithmetic and copies ran while one was open for 0% of the time, Pallas kernels for 0%

profile of v1, /device:TPU:0, one launch (start us, length us, event | category | flops | bytes accessed | tf_op | source)
XLA Modules:
  0.0 1835.6 jit_solution(16731971945219847615)
XLA Ops:
  8.7 5.9 gather_fusion
  14.6 1.3 convert_select_fusion
  15.9 549.4 %all-reduce.3.cloned.1.call-done = f32[1024,256]{1,0:T(8,128)} async-done(((f32[1024,256]{1,0:T(8,128)}), f32[1024,256]{1,0:T(8,128)}) %all-reduce.3.cloned.1.call-update) | async-done | bytes 1048592 | tf_op jit(solution)/shard_map/psum | solution.py:12
  565.3 32.0 %all-reduce.4 = bf16[1024,256]{1,0:T(8,128)(2,1)S(1)} all-reduce(f32[1024,256]{1,0:T(8,128)} %all-reduce.3.cloned.1.call-done), channel_id=1, replica_groups=mesh['grid'=64,'col'=2] {'col'}, use_global_device_ids=true, to_apply=%region_1.2 | all-reduce | flops 262144 | bytes 1572864 | tf_op jit(solution)/shard_map/psum | solution.py:13
  597.3 19.9 %while.10 = (s32[]{:T(128)}, bf16[6,1152,1024]{2,1,0:T(8,128)(2,1)}, bf16[6,1152,256]{2,1,0:T(8,128)(2,1)}, bf16[1024,256]{1,0:T(8,128)(2,1)S(1)}, s32[]{:T(128)}) while((s32[]{:T(128)}, bf16[6,1152,1024]{2,1,0:T(8,128)(2,1)}, bf16[6,1152,256]{2,1,0:T(8,128)(2,1)}, bf16[1024,256]{1,0:T(8,128)(2,1)S(1)}, s32[]{:T(128)}) %tuple.30), condition=%wide.region_3.4_spmd, body=%wide.region_2.3_spmd.sunk | while | flops 607518720 | bytes 3474501 | solution.py:82
  597.3 3.3 fusion.234
  600.6 3.3 fusion.234
  603.9 3.3 fusion.234
  607.3 3.4 fusion.234
  610.6 3.3 fusion.234
  613.9 3.3 fusion.234
  617.2 11.7 convolution_bitcast_fusion
  629.0 9.1 all_to_all.26
  638.1 9.7 all-to-all-start
  648.1 3.1 fusion.18
  651.2 81.1 %all-to-all-done = f32[128,2,6912]{2,1,0:T(2,128)} async-done(((f32[128,2,6912]{2,1,0:T(2,128)}), f32[128,2,6912]{2,1,0:T(2,128)}, u32[]{:S(2)}, u32[]{:S(2)}) %all-to-all-start) | async-done | bytes 7077920 | tf_op jit(solution)/shard_map/all_to_all | solution.py:89
  732.3 6.4 copy.15
  738.6 10.6 reshape.103
  749.2 11.3 fusion.39
  760.5 21.2 %fusion.57 = f32[2,96,96,96]{2,3,1,0:T(8,128)S(1)} fusion(f32[2,96,96,96]{3,2,1,0:T(8,128)S(1)} %copy-done.6), kind=kOutput, calls=%fused_computation.66 | convolution fusion | flops 2038514688 | bytes 14155776 | tf_op jit(solution)/shard_map/kn,cxyn->cxyk/dot_general | solution.py:28
  781.8 8.8 fusion.55
  790.6 10.5 fusion.36
  801.0 19.2 %subtract_bitcast_fusion.1 = f32[2,96,96,96]{2,3,1,0:T(8,128)} fusion(f32[2,96,96,96]{3,2,1,0:T(8,128)} %fusion.36, f32[2,96,96,96]{3,2,1,0:T(8,128)S(1)} %fusion.39), kind=kOutput, calls=%fused_computation.21 | convolution fusion | flops 2042053632 | bytes 21233664 | tf_op jit(solution)/shard_map/kn,cxnz->cxkz/dot_general | solution.py:28
  820.2 17.8 add_bitcast_fusion.1
  838.0 12.4 copy.18
  850.3 12.4 copy.21
  862.7 13.4 fusion.48
  876.1 10.2 fusion.53
  886.3 11.3 bitcast_multiply_fusion
  897.6 15.4 bitcast_multiply_fusion.1
  913.0 10.3 fusion.50
  923.3 8.8 fusion.44
  932.1 10.6 add_bitcast_fusion
  942.8 12.4 copy.31
  955.2 26.4 %fusion.41 = f32[2,96,96,96]{2,3,1,0:T(8,128)} fusion(f32[2,96,96,96]{2,3,1,0:T(8,128)} %copy.31), kind=kOutput, calls=%fused_computation.50 | convolution fusion | flops 2038514688 | bytes 14155776 | tf_op jit(solution)/shard_map/kn,cxnz->cxkz/dot_general | solution.py:28
  981.6 23.6 %fusion.30 = f32[2,96,96,96]{2,3,1,0:T(8,128)} fusion(f32[2,96,96,96]{2,3,1,0:T(8,128)S(1)} %copy-done.3), kind=kOutput, calls=%fused_computation.39 | convolution fusion | flops 2038514688 | bytes 14155776 | tf_op jit(solution)/shard_map/kn,cxnz->cxkz/dot_general | solution.py:28
  1005.3 10.6 subtract_bitcast_fusion
  1015.9 12.5 copy.30
  1028.4 24.6 %fusion.28 = f32[2,96,96,96]{2,3,1,0:T(8,128)S(1)} fusion(f32[2,96,96,96]{2,3,1,0:T(8,128)} %copy.30), kind=kOutput, calls=%fused_computation.37 | convolution fusion | flops 2038514688 | bytes 14155776 | tf_op jit(solution)/shard_map/kn,cxnz->cxkz/dot_general | solution.py:28
  1053.0 23.4 %fusion.46 = f32[2,96,96,96]{2,3,1,0:T(8,128)} fusion(f32[2,96,96,96]{2,3,1,0:T(8,128)S(1)} %copy-done.4), kind=kOutput, calls=%fused_computation.55 | convolution fusion | flops 2038514688 | bytes 14155776 | tf_op jit(solution)/shard_map/kn,cxnz->cxkz/dot_general | solution.py:28
  1076.4 10.2 fusion.7
  1086.7 15.9 multiply_convert_fusion
  1102.6 7.8 all_to_all.29
  1110.3 5.6 copy.24
  1116.0 55.8 %all_to_all.35 = bf16[2,128,6912]{2,0,1:T(2,128)(2,1)} all-to-all(bf16[2,128,6912]{2,0,1:T(2,128)(2,1)S(1)} %copy.24), channel_id=1, replica_groups=mesh['grid'=64,'col'=2] {'grid','col'}, dimensions={1} | all-to-all | bytes 7077888 | tf_op jit(solution)/shard_map/all_to_all | solution.py:92
  1171.8 8.3 all_to_all.32
  1180.1 10.9 convolution_multiply_fusion.1
  1191.0 637.2 %reduce-scatter.2.cloned.1.call-done = f32[8,256]{1,0:T(8,128)} async-done(((f32[1024,256]{1,0:T(8,128)}), f32[8,256]{1,0:T(8,128)}) %reduce-scatter.2.cloned.1.call-update) | async-done | bytes 8208 | tf_op jit(solution)/shard_map/reduce_scatter | solution.py:94
  (49 shorter events, 1.9 us)
Async XLA Ops:
  7.2 610.1 %copy-start = (bf16[1024,256]{1,0:T(8,128)(2,1)S(1)}, bf16[1024,256]{1,0:T(8,128)(2,1)}, u32[]{:S(2)}) copy-start(bf16[1024,256]{1,0:T(8,128)(2,1)} %param.7) | copy-start | bytes 1572868
  7.2 558.1 %all-reduce.3.cloned.1.call-start = ((), (), s32[]{:S(2)}) async-start(), calls=%async_computation.3 | async-start | bytes 2097152 | tf_op jit(solution)/shard_map/psum | solution.py:12
  638.1 94.2 %all-to-all-start = ((f32[128,2,6912]{2,1,0:T(2,128)}), f32[128,2,6912]{2,1,0:T(2,128)}, u32[]{:S(2)}, u32[]{:S(2)}) async-start(f32[128,2,6912]{2,1,0:T(2,128)} %all_to_all.26), calls=%async_computation | async-start | bytes 14155776 | tf_op jit(solution)/shard_map/all_to_all | solution.py:89
  647.7 1180.5 %reduce-scatter.2.cloned.1.call-start = ((), (), s32[]{:S(2)}) async-start(), calls=%async_computation.4 | async-start | bytes 1056768 | tf_op jit(solution)/shard_map/reduce_scatter | solution.py:94
  749.2 11.3 copy-start.6
  862.7 13.4 copy-start.5
  862.7 23.6 %slice-start = ((s8[4718592]{0:T(1024)(128)(4,1)}), s8[4194304]{0:T(1024)(128)(4,1)S(1)}, s32[]{:S(2)}) async-start(s8[4718592]{0:T(1024)(128)(4,1)} %bitcast.108), calls=%async_computation.5 | async-start | bytes 8388608
  876.1 10.2 slice-start.1
  897.6 25.7 %copy-start.2 = (f32[2,96,96,96]{1,3,2,0:T(8,128)}, f32[2,96,96,96]{1,3,2,0:T(8,128)S(1)}, u32[]{:S(2)}) copy-start(f32[2,96,96,96]{1,3,2,0:T(8,128)S(1)} %bitcast_multiply_fusion) | copy-start | bytes 21233668
  955.1 26.4 %copy-start.3 = (f32[2,96,96,96]{2,3,1,0:T(8,128)S(1)}, f32[2,96,96,96]{2,3,1,0:T(8,128)}, u32[]{:S(2)}) copy-start(f32[2,96,96,96]{2,3,1,0:T(8,128)} %copy.31) | copy-start | bytes 21233668
  955.1 50.1 %slice-start.2 = ((s8[9437184]{0:T(1024)(128)(4,1)}), s8[4194304]{0:T(1024)(128)(4,1)S(1)}, s32[]{:S(2)}) async-start(s8[9437184]{0:T(1024)(128)(4,1)} %bitcast.110), calls=%async_computation.7 | async-start | bytes 8388608
  955.2 50.1 %slice-start.3 = ((s8[9437184]{0:T(1024)(128)(4,1)}), s8[4194304]{0:T(1024)(128)(4,1)S(1)}, s32[]{:S(2)}) async-start(s8[9437184]{0:T(1024)(128)(4,1)} %bitcast.110), calls=%async_computation.8 | async-start | bytes 8388608
  955.2 50.1 %slice-start.5 = ((s8[9437184]{0:T(1024)(128)(4,1)}), s8[4194304]{0:T(1024)(128)(4,1)S(1)}, s32[]{:S(2)}) async-start(s8[9437184]{0:T(1024)(128)(4,1)} %bitcast.112), calls=%async_computation.10 | async-start | bytes 8388608
  955.2 50.1 %slice-start.6 = ((s8[9437184]{0:T(1024)(128)(4,1)}), s8[4194304]{0:T(1024)(128)(4,1)S(1)}, s32[]{:S(2)}) async-start(s8[9437184]{0:T(1024)(128)(4,1)} %bitcast.112), calls=%async_computation.11 | async-start | bytes 8388608
  981.6 23.7 %slice-start.4 = ((s8[9437184]{0:T(1024)(128)(4,1)}), s8[1048576]{0:T(1024)(128)(4,1)S(1)}, s32[]{:S(2)}) async-start(s8[9437184]{0:T(1024)(128)(4,1)} %bitcast.110), calls=%async_computation.9 | async-start | bytes 2097152
  981.6 23.7 %slice-start.7 = ((s8[9437184]{0:T(1024)(128)(4,1)}), s8[1048576]{0:T(1024)(128)(4,1)S(1)}, s32[]{:S(2)}) async-start(s8[9437184]{0:T(1024)(128)(4,1)} %bitcast.112), calls=%async_computation.12 | async-start | bytes 2097152
  1028.4 24.6 %copy-start.4 = (f32[2,96,96,96]{2,3,1,0:T(8,128)S(1)}, f32[2,96,96,96]{2,3,1,0:T(8,128)}, u32[]{:S(2)}) copy-start(f32[2,96,96,96]{2,3,1,0:T(8,128)} %copy.30) | copy-start | bytes 21233668
  1028.4 48.0 %slice-start.8 = ((s8[9437184]{0:T(1024)(128)(4,1)}), s8[4194304]{0:T(1024)(128)(4,1)S(1)}, s32[]{:S(2)}) async-start(s8[9437184]{0:T(1024)(128)(4,1)} %bitcast.114), calls=%async_computation.13 | async-start | bytes 8388608
  1028.4 48.0 %slice-start.9 = ((s8[9437184]{0:T(1024)(128)(4,1)}), s8[4194304]{0:T(1024)(128)(4,1)S(1)}, s32[]{:S(2)}) async-start(s8[9437184]{0:T(1024)(128)(4,1)} %bitcast.114), calls=%async_computation.14 | async-start | bytes 8388608
  1053.0 23.4 %slice-start.10 = ((s8[9437184]{0:T(1024)(128)(4,1)}), s8[1048576]{0:T(1024)(128)(4,1)S(1)}, s32[]{:S(2)}) async-start(s8[9437184]{0:T(1024)(128)(4,1)} %bitcast.114), calls=%async_computation.15 | async-start | bytes 2097152
  1171.8 656.4 %copy-start.1 = (bf16[1024,256]{1,0:T(8,128)(2,1)S(1)}, bf16[1024,256]{1,0:T(8,128)(2,1)}, u32[]{:S(2)}) copy-start(bf16[1024,256]{1,0:T(8,128)(2,1)} %param.7) | copy-start | bytes 1572868
Sparse Core Ops, SparseCore 0:
  16.1 549.1 all-reduce.2
  1191.1 637.0 reduce-scatter.1
